TPU v7x, 256 devices: a whole 4x4x8 slice. The times are simulated.
256 devices in a mesh: tile: 64 (over z, y, core), frame: 4 (over x).
Axes of the slice: x: 4, y: 4, z: 8, core: 2. Of those that a mesh axis runs over, the one named last changes fastest.
Arguments:
- feats: bfloat16 [4, 16384, 256], P('frame', 'tile'), may hold values from -6 to 6
- routes: int32 [4, 64, 64], P('frame'), may hold values from 0 to 63, as said below
- interp: bfloat16 [4, 64, 16384, 128], P('frame', None, 'tile'), may hold values from -0.5 to 0.5
- w_value: bfloat16 [256, 256], replicated, may hold values from -0.375 to 0.375
- w_attn: bfloat16 [256, 64], replicated, may hold values from -48 to 48
- w_out: bfloat16 [256, 256], replicated, may hold values from -0.375 to 0.375
- grad_out: bfloat16 [4, 16384, 256], P('frame', 'tile'), may hold values from -6 to 6
Outputs:
- grad_feats: bfloat16 [4, 16384, 256], P('frame', 'tile')
- grad_w_value: float32 [256, 256], replicated
- grad_w_attn: float32 [256, 64], replicated
- grad_w_out: float32 [256, 256], replicated
Inputs may be any that keep to these rules, and one draw needn't show every extreme that they name: `routes`: within one frame a reader tile names any one owner tile in at most 2 of its 64 columns; in every frame some owner tile is named in exactly 2 columns by every reader tile.
All inputs are finite; a program needn't handle non-finite values.
Results may differ from a plain program's by a relative error of at most 0.022.
Values may be sent and summed in bfloat16 or wider, within the bound.
A program may use at most 128 MiB of HBM per device.

v0:
```python
import math
import jax
import jax.numpy as jnp
from jax import lax
from jax.sharding import PartitionSpec as P

H = 8
L = 2
P_SIZE = 4


def per_device(feats, routes, interp, w_value, w_attn, w_out, grad_out):
    inputs_now = feats[0]
    grads_now = grad_out[0]
    tile_weights = interp[0]
    routes_now = routes[0]
    tile_count = lax.axis_size("tile")
    myself = lax.axis_index("tile")
    row_count = inputs_now.shape[0]
    model_width = inputs_now.shape[1]
    column_count = tile_weights.shape[0]
    cell_count = tile_weights.shape[2]
    head_count = H
    level_count = L
    point_count = P_SIZE
    group_width = level_count * point_count
    head_dim = model_width // head_count
    capacity = max(2, 2 * column_count // tile_count)
    column = jnp.arange(column_count, dtype=jnp.int32)
    head_of = column // group_width
    level_of = column // point_count % level_count
    lookup_index = level_of * head_count + head_of
    my_routes = lax.dynamic_index_in_dim(routes_now, myself, 0, keepdims=False)
    earlier = (my_routes[None, :] == my_routes[:, None]) & (column[None, :] < column[:, None])
    ranking = jnp.sum(earlier.astype(jnp.int32), axis=1)
    slot_index = my_routes * capacity + ranking
    aimed = routes_now == myself
    ordering = jnp.cumsum(aimed.astype(jnp.int32), axis=1) - 1
    slot_range = jnp.arange(capacity, dtype=jnp.int32)
    picked = aimed[:, None, :] & (ordering[:, None, :] == slot_range[None, :, None])
    filled = jnp.any(picked, axis=2)
    chosen = jnp.sum(jnp.where(picked, lookup_index[None, None, :], 0), axis=2)
    values = jnp.dot(inputs_now, w_value, preferred_element_type=jnp.float32).astype(jnp.bfloat16)
    lookup = values.reshape(level_count, cell_count, head_count, head_dim).transpose(0, 2, 3, 1)
    lookup = lookup.reshape(level_count * head_count, head_dim, cell_count)
    empty = jnp.zeros((column_count, head_dim, cell_count), jnp.bfloat16)
    pieces = lax.all_gather(lookup[None], "tile", axis=0, tiled=True)
    owner_count = pieces.shape[0]
    inside = (my_routes >= 0) & (my_routes < owner_count)
    found = pieces[jnp.clip(my_routes, 0, owner_count - 1), lookup_index]
    fetched = jnp.where(inside[:, None, None], found, empty)
    sampled = jnp.einsum("jdc,jqc->jdq", fetched, tile_weights, preferred_element_type=jnp.float32)
    logits = jnp.dot(inputs_now, w_attn, preferred_element_type=jnp.float32)
    attn = jax.nn.softmax(logits.reshape(row_count, head_count, group_width), axis=-1).reshape(
        row_count, column_count
    )
    attn_heads = attn.T.reshape(head_count, group_width, 1, row_count)
    sampled_heads = sampled.reshape(head_count, group_width, head_dim, row_count)
    mixed = (
        jnp.sum(attn_heads * sampled_heads, axis=1)
        .reshape(model_width, row_count)
        .T.astype(jnp.bfloat16)
    )
    grad_mixed = jnp.dot(grads_now, w_out.T, preferred_element_type=jnp.float32)
    grad_mixed_heads = grad_mixed.T.reshape(head_count, 1, head_dim, row_count)
    grad_attn = jnp.sum(grad_mixed_heads * sampled_heads, axis=2).reshape(column_count, row_count).T
    grad_attn = grad_attn.reshape(row_count, head_count, group_width)
    attn_query = attn.reshape(row_count, head_count, group_width)
    inner_term = jnp.sum(attn_query * grad_attn, axis=-1, keepdims=True)
    grad_logits = (
        (attn_query * (grad_attn - inner_term))
        .reshape(row_count, column_count)
        .astype(jnp.bfloat16)
    )
    grad_sampled = (
        (attn_heads * grad_mixed_heads)
        .reshape(column_count, head_dim, row_count)
        .astype(jnp.bfloat16)
    )
    contrib = jnp.einsum(
        "jdq,jqc->jdc", grad_sampled, tile_weights, preferred_element_type=jnp.float32
    )
    outgoing = (
        jnp.zeros((tile_count * capacity, head_dim, cell_count), jnp.float32)
        .at[slot_index]
        .set(contrib)
    )
    returned = lax.all_to_all(
        outgoing.reshape(tile_count, capacity, head_dim, cell_count).astype(jnp.bfloat16),
        "tile",
        split_axis=0,
        concat_axis=0,
        tiled=True,
    ).astype(jnp.float32)
    table_range = jnp.arange(level_count * head_count, dtype=jnp.int32)
    member = (chosen.reshape(-1)[None, :] == table_range[:, None]) & filled.reshape(-1)[None, :]
    grad_lookup = jnp.dot(
        member.astype(jnp.float32),
        returned.reshape(tile_count * capacity, head_dim * cell_count),
        precision=lax.Precision.HIGHEST,
    )
    grad_values = grad_lookup.reshape(level_count, head_count, head_dim, cell_count).transpose(
        0, 3, 1, 2
    )
    grad_values = grad_values.reshape(row_count, model_width).astype(jnp.bfloat16)
    grad_query = jnp.dot(grad_logits, w_attn.T, preferred_element_type=jnp.float32)
    part_attn = jnp.dot(inputs_now.T, grad_logits, preferred_element_type=jnp.float32)
    part_out = jnp.dot(mixed.T, grads_now, preferred_element_type=jnp.float32)
    grad_inputs = grad_query + jnp.dot(grad_values, w_value.T, preferred_element_type=jnp.float32)
    part_value = jnp.dot(inputs_now.T, grad_values, preferred_element_type=jnp.float32)
    totals = lax.psum((part_value, part_attn, part_out), ("tile", "frame"))
    factor = 1.0 / math.sqrt(tile_count * lax.axis_size("frame") * row_count)
    return (
        grad_inputs.astype(jnp.bfloat16)[None],
        totals[0] * factor,
        totals[1] * factor,
        totals[2] * factor,
    )


def solution(mesh):
    in_specs = (
        P("frame", "tile", None),
        P("frame", None, None),
        P("frame", None, "tile", None),
        P(),
        P(),
        P(),
        P("frame", "tile", None),
    )
    out_specs = (P("frame", "tile", None), P(), P(), P())
    return jax.shard_map(
        per_device, mesh=mesh, in_specs=in_specs, out_specs=out_specs, check_vma=False
    )
```

profile of v0, /device:TPU:1, one launch (start us, length us, event | category | flops | bytes accessed | tf_op | source)
XLA Modules:
  0.0 408.1 jit_solution(1071865935539580949)
XLA Ops:
  7.2 0.0 copy-start
  7.2 0.0 all-gather.2.cloned.1.call-start
  7.2 0.8 copy-done
  8.1 1.1 convolution_convert_fusion
  9.2 0.1 copy.28
  9.3 0.7 copy.29
  10.0 0.0 all-gather.2.cloned.1.call-update
  10.0 0.7 compare_and_fusion
  10.7 0.2 convert_reduce_fusion
  10.9 1.0 fusion.13
  11.9 1.2 fusion.25
  13.1 85.5 %all-gather.2.cloned.1.call-done = bf16[64,16,32,128]{3,2,1,0:T(8,128)(2,1)} async-done(((bf16[1,16,32,128]{3,2,1,0:T(8,128)(2,1)}), bf16[64,16,32,128]{3,2,1,0:T(8,128)(2,1)}) %all-gather.2.cloned.1.call-update) | async-done | bytes 8388624 | tf_op jit(solution)/shard_map/all_gather | solution.py:47
  98.7 4.1 %gather_fusion = bf16[64,32,128]{2,1,0:T(8,128)(2,1)S(1)} fusion(bf16[64,16,32,128]{3,2,1,0:T(8,128)(2,1)} %all-gather.2.cloned.1.call-done, s32[64]{0:T(128)S(1)} %get-tuple-element.30), kind=kCustom, calls=%fused_computation | custom fusion | bytes 1049088 | tf_op jit(solution)/shard_map/gather | solution.py:50
  102.8 0.0 copy-start.1
  102.8 5.2 %fusion.8 = (bf16[64,32,256]{2,1,0:T(8,128)(2,1)S(1)}, f32[64,256]{1,0:T(8,128)S(1)}, f32[64,32,256]{2,1,0:T(8,128)}) fusion(f32[64,256]{1,0:T(8,128)S(1)} %bitcast.145, f32[8,32,256]{2,1,0:T(8,128)S(1)} %fusion.25, bf16[1,64,256,128]{3,2,1,0:T(8,128)(2,1)} %param.9, bf16[64,32,128]{2,1,0:T(8,128)(2,1)S(1)} %gather_fusion, ...), kind=kOutput, calls=%fused_computation.12 | convolution fusion | flops 136560640 | bytes 8257600 | tf_op jit(solution)/shard_map/jdc,jqc->jdq/dot_general | solution.py:52
  108.0 0.0 copy-done.1
  108.0 0.7 fusion.3
  108.7 0.3 broadcast_in_dim.30
  109.0 2.5 scatter_fusion
  111.5 0.0 copy-start.5
  111.5 1.2 convert_element_type.58
  112.7 0.0 copy-start.2
  112.7 6.4 %all-to-all-start = ((bf16[64,2,32,128]{3,2,1,0:T(8,128)(2,1)}), bf16[64,2,32,128]{3,2,1,0:T(8,128)(2,1)S(1)}, u32[]{:S(2)}, u32[]{:S(2)}) async-start(bf16[64,2,32,128]{3,2,1,0:T(8,128)(2,1)} %bitcast.26), calls=%async_computation | async-start | bytes 2097152 | tf_op jit(solution)/shard_map/all_to_all | solution.py:88
  119.1 0.0 all-reduce.3.cloned.1.call-start
  119.1 0.0 copy-done.5
  119.2 0.2 reduce_window_sum.11
  119.4 0.1 select_reduce_fusion
  119.5 0.1 copy.30
  119.6 0.1 eq.77
  119.8 0.1 fusion.45
  119.9 0.1 copy.31
  120.0 0.2 and.128
  120.2 0.0 copy-done.2
  120.2 0.3 multiply_reduce_fusion
  120.5 0.8 convolution_bitcast_fusion.1
  121.3 1.8 fusion.27
  123.1 24.0 %all-to-all-done = bf16[64,2,32,128]{3,2,1,0:T(8,128)(2,1)S(1)} async-done(((bf16[64,2,32,128]{3,2,1,0:T(8,128)(2,1)}), bf16[64,2,32,128]{3,2,1,0:T(8,128)(2,1)S(1)}, u32[]{:S(2)}, u32[]{:S(2)}) %all-to-all-start) | async-done | bytes 1048608 | tf_op jit(solution)/shard_map/all_to_all | solution.py:88
  147.1 0.5 copy.50
  147.5 0.0 copy-start.6
  147.5 0.0 copy-start.3
  147.5 0.7 copy.32
  148.2 0.4 fusion.11
  148.6 0.2 copy.33
  148.8 0.9 convolution_bitcast_fusion
  149.7 0.0 all-reduce.3.cloned.1.call-update
  149.7 0.0 copy-done.6
  149.7 0.2 fusion.19
  149.9 0.0 copy-done.3
  150.0 0.9 fusion.10
  150.8 247.0 %all-reduce.3.cloned.1.call-done = (f32[256,256]{0,1:T(8,128)}, f32[256,64]{0,1:T(8,128)}, f32[256,256]{0,1:T(8,128)}) async-done(((f32[256,256]{0,1:T(8,128)}, f32[256,64]{0,1:T(8,128)}, f32[256,256]{0,1:T(8,128)}), (f32[256,256]{0,1:T(8,128)}, f32[256,64]{0,1:T(8,128)}, f32[256,256]{0,1:T(8,128)})) %all-reduce.3.cloned.1.call-update) | async-done | bytes 589840 | tf_op jit(solution)/shard_map/psum | solution.py:111
  397.8 0.0 copy-start.4
  397.8 1.1 broadcast_multiply_fusion
  398.9 0.8 copy.35
  399.8 0.8 copy.36
  400.6 0.0 copy-done.4
  400.6 0.6 broadcast_multiply_fusion.2
  (6 shorter events, 0.1 us)
Async XLA Ops:
  7.2 0.9 copy-start
  7.2 91.5 %all-gather.2.cloned.1.call-start = ((), (), s32[]{:S(2)}) async-start(), calls=%async_computation.1 | async-start | bytes 8519680 | tf_op jit(solution)/shard_map/all_gather | solution.py:47
  102.8 5.3 %copy-start.1 = (bf16[1,64,256,128]{3,2,1,0:T(8,128)(2,1)S(1)}, bf16[1,64,256,128]{3,2,1,0:T(8,128)(2,1)}, u32[]{:S(2)}) copy-start(bf16[1,64,256,128]{3,2,1,0:T(8,128)(2,1)} %param.9) | copy-start | bytes 12582916
  111.5 7.6 %copy-start.5 = (s32[1,64,64]{2,1,0:T(8,128)S(1)}, s32[1,64,64]{2,1,0:T(8,128)}, u32[]{:S(2)}) copy-start(s32[1,64,64]{2,1,0:T(8,128)} %param.8) | copy-start | bytes 49156
  112.7 7.5 %copy-start.2 = (f32[64,32,256]{2,1,0:T(8,128)S(1)}, f32[64,32,256]{2,1,0:T(8,128)}, u32[]{:S(2)}) copy-start(f32[64,32,256]{2,1,0:T(8,128)} %get-tuple-element.31) | copy-start | bytes 6291460
  112.7 34.4 %all-to-all-start = ((bf16[64,2,32,128]{3,2,1,0:T(8,128)(2,1)}), bf16[64,2,32,128]{3,2,1,0:T(8,128)(2,1)S(1)}, u32[]{:S(2)}, u32[]{:S(2)}) async-start(bf16[64,2,32,128]{3,2,1,0:T(8,128)(2,1)} %bitcast.26), calls=%async_computation | async-start | bytes 2097152 | tf_op jit(solution)/shard_map/all_to_all | solution.py:88
  119.1 278.7 %all-reduce.3.cloned.1.call-start = ((), (), s32[]{:S(2)}) async-start(), calls=%async_computation.2 | async-start | bytes 1179648 | tf_op jit(solution)/shard_map/psum | solution.py:111
  147.5 2.2 copy-start.6
  147.5 2.4 copy-start.3
  397.8 2.8 copy-start.4
Sparse Core Ops, SparseCore 0:
  11.4 87.2 all-gather.1
  149.8 247.9 all-reduce.2
where the time goes:
time: 408 us
  waiting for transfers between devices  357 us (88%)
  between operations  14.3 us (4%)
  matrix products  14.2 us (3%)
  local copies, waits for them, and re-layouts  12 us (3%)
  starting transfers between devices  6.44 us (2%)
  other arithmetic  4.6 us (1%)
    psum x1, waiting for transfers between devices, per_device(): totals = lax.psum((part_value, part_attn, part_out), ('tile', 'frame'))  247 us
    all_gather x1, waiting for transfers between devices, per_device(): pieces = lax.all_gather(lookup[None], 'tile', axis=0, tiled=True)  85.5 us
    all_to_all x1, waiting for transfers between devices, per_device(): lax.all_to_all(outgoing.reshape(tile_count, capacity, head_dim, cell_coun...  24 us
  transfers between devices with their start and end apart: 3, of which 3 were waited for; matrix products, arithmetic and copies ran while one was open for 2% of the time, Pallas kernels for 0%

commit v1 on v0

--- a/solution.py
+++ b/solution.py
@@ -44,7 +44,9 @@
     lookup = values.reshape(level_count, cell_count, head_count, head_dim).transpose(0, 2, 3, 1)
     lookup = lookup.reshape(level_count * head_count, head_dim, cell_count)
     empty = jnp.zeros((column_count, head_dim, cell_count), jnp.bfloat16)
-    pieces = lax.all_gather(lookup[None], "tile", axis=0, tiled=True)
+    pieces = jnp.concatenate(
+        lax.all_to_all(jnp.stack([lookup[None]] * lax.axis_size("tile")), "tile", 0, 0), axis=0
+    )
     owner_count = pieces.shape[0]
     inside = (my_routes >= 0) & (my_routes < owner_count)
     found = pieces[jnp.clip(my_routes, 0, owner_count - 1), lookup_index]

time: 408 us -> 524 us (1.28)
  waiting for transfers between devices: 357 us -> 453 us
  starting transfers between devices: 6.44 us -> 23.7 us
    all_to_all x0 -> x1, waiting for transfers between devices: none -> 182 us  [per_device(): lax.all_to_all(jnp.stack([lookup[None]] * lax.axis_size('tile')), 'tile',...]
    all_gather x1 -> x0, waiting for transfers between devices: 85.5 us -> none  [per_device(): pieces = lax.all_gather(lookup[None], 'tile', axis=0, tiled=True)]
    all_to_all x0 -> x1, starting transfers between devices: none -> 13.5 us  [per_device(): lax.all_to_all(jnp.stack([lookup[None]] * lax.axis_size('tile')), 'tile',...]
  transfers between devices with their start and end apart: 3 -> 3, of which waited for: 3 -> 3; matrix products, arithmetic and copies ran while one was open for 2% -> 1% of each run, Pallas kernels for 0% -> 0%
where the time goes in v1:
time: 524 us
  waiting for transfers between devices  453 us (86%)
  starting transfers between devices  23.7 us (5%)
  local copies, waits for them, and re-layouts  16.7 us (3%)
  between operations  14.3 us (3%)
  matrix products  12.5 us (2%)
    psum x1, waiting for transfers between devices, per_device(): totals = lax.psum((part_value, part_attn, part_out), ('tile', 'frame'))  247 us
    all_to_all x1, waiting for transfers between devices, per_device(): lax.all_to_all(jnp.stack([lookup[None]] * lax.axis_size('tile')), 'tile',...  182 us
    all_to_all x1, waiting for transfers between devices, per_device(): lax.all_to_all(outgoing.reshape(tile_count, capacity, head_dim, cell_coun...  24 us
    all_to_all x1, starting transfers between devices, per_device(): lax.all_to_all(jnp.stack([lookup[None]] * lax.axis_size('tile')), 'tile',...  13.5 us
  transfers between devices with their start and end apart: 3, of which 3 were waited for; matrix products, arithmetic and copies ran while one was open for 1% of the time, Pallas kernels for 0%

profile of v1, /device:TPU:1, one launch (start us, length us, event | category | flops | bytes accessed | tf_op | source)
XLA Modules:
  0.0 523.7 jit_solution(17276451017104422664)
XLA Ops:
  7.2 0.0 copy-start
  7.2 0.9 copy-done
  8.1 1.1 convolution_convert_fusion
  9.2 0.1 copy.21
  9.3 5.2 stack.3
  14.6 0.0 copy-start.7
  14.6 0.0 copy-start.8
  14.6 0.0 copy-start.4
  14.6 0.0 copy-start.5
  14.6 13.5 %all-to-all-start = ((bf16[64,1,16,32,128]{4,3,2,1,0:T(8,128)(2,1)}), bf16[64,1,16,32,128]{4,3,2,1,0:T(8,128)(2,1)}, u32[]{:S(2)}, u32[]{:S(2)}) async-start(bf16[64,1,16,32,128]{4,3,2,1,0:T(8,128)(2,1)} %stack.3), calls=%async_computation | async-start | bytes 16777216 | tf_op jit(solution)/shard_map/all_to_all | solution.py:48
  28.1 0.0 copy-done.7
  28.1 0.2 convert_reduce_fusion
  28.3 0.0 copy-done.8
  28.3 0.2 fusion.13
  28.6 0.0 copy-done.4
  28.6 0.0 copy-done.5
  28.6 0.2 fusion.25
  28.8 181.6 %all-to-all-done = bf16[64,1,16,32,128]{4,3,2,1,0:T(8,128)(2,1)} async-done(((bf16[64,1,16,32,128]{4,3,2,1,0:T(8,128)(2,1)}), bf16[64,1,16,32,128]{4,3,2,1,0:T(8,128)(2,1)}, u32[]{:S(2)}, u32[]{:S(2)}) %all-to-all-start) | async-done | bytes 8388640 | tf_op jit(solution)/shard_map/all_to_all | solution.py:48
  210.5 4.1 gather_fusion
  214.6 0.0 copy-start.1
  214.6 5.2 %fusion.8 = (bf16[64,32,256]{2,1,0:T(8,128)(2,1)S(1)}, f32[64,256]{1,0:T(8,128)S(1)}, f32[64,32,256]{2,1,0:T(8,128)}) fusion(f32[64,256]{1,0:T(8,128)S(1)} %bitcast.146, f32[8,32,256]{2,1,0:T(8,128)S(1)} %fusion.25, bf16[1,64,256,128]{3,2,1,0:T(8,128)(2,1)} %param.9, bf16[64,32,128]{2,1,0:T(8,128)(2,1)S(1)} %gather_fusion, ...), kind=kOutput, calls=%fused_computation.12 | convolution fusion | flops 136560640 | bytes 8257600 | tf_op jit(solution)/shard_map/jdc,jqc->jdq/dot_general | solution.py:54
  219.8 0.0 copy-done.1
  219.8 0.7 fusion.3
  220.5 0.3 broadcast_in_dim.30
  220.8 2.5 scatter_fusion
  223.3 1.2 convert_element_type.58
  224.5 0.0 copy-start.2
  224.5 10.2 %all-to-all-start.1 = ((bf16[64,2,32,128]{3,2,1,0:T(8,128)(2,1)}), bf16[64,2,32,128]{3,2,1,0:T(8,128)(2,1)S(1)}, u32[]{:S(2)}, u32[]{:S(2)}) async-start(bf16[64,2,32,128]{3,2,1,0:T(8,128)(2,1)} %bitcast.27), calls=%async_computation.1 | async-start | bytes 2097152 | tf_op jit(solution)/shard_map/all_to_all | solution.py:90
  234.7 0.0 all-reduce.3.cloned.1.call-start
  234.8 0.2 reduce_window_sum.11
  235.0 0.1 select_reduce_fusion
  235.1 0.1 copy.23
  235.2 0.1 eq.77
  235.4 0.1 fusion.45
  235.5 0.1 copy.24
  235.6 0.2 and.128
  235.8 0.0 copy-done.2
  235.8 0.3 multiply_reduce_fusion
  236.1 0.8 convolution_bitcast_fusion.1
  236.9 1.8 fusion.27
  238.7 24.0 %all-to-all-done.1 = bf16[64,2,32,128]{3,2,1,0:T(8,128)(2,1)S(1)} async-done(((bf16[64,2,32,128]{3,2,1,0:T(8,128)(2,1)}), bf16[64,2,32,128]{3,2,1,0:T(8,128)(2,1)S(1)}, u32[]{:S(2)}, u32[]{:S(2)}) %all-to-all-start.1) | async-done | bytes 1048608 | tf_op jit(solution)/shard_map/all_to_all | solution.py:90
  262.7 0.5 copy.43
  263.1 0.0 copy-start.9
  263.2 0.0 copy-start.3
  263.2 0.7 copy.25
  263.8 0.4 fusion.11
  264.2 0.2 copy.26
  264.4 0.9 convolution_bitcast_fusion
  265.3 0.0 all-reduce.3.cloned.1.call-update
  265.3 0.0 copy-done.9
  265.3 0.2 fusion.19
  265.6 0.0 copy-done.3
  265.6 0.9 fusion.10
  266.5 247.0 %all-reduce.3.cloned.1.call-done = (f32[256,256]{0,1:T(8,128)}, f32[256,64]{0,1:T(8,128)}, f32[256,256]{0,1:T(8,128)}) async-done(((f32[256,256]{0,1:T(8,128)}, f32[256,64]{0,1:T(8,128)}, f32[256,256]{0,1:T(8,128)}), (f32[256,256]{0,1:T(8,128)}, f32[256,64]{0,1:T(8,128)}, f32[256,256]{0,1:T(8,128)})) %all-reduce.3.cloned.1.call-update) | async-done | bytes 589840 | tf_op jit(solution)/shard_map/psum | solution.py:113
  513.5 0.0 copy-start.6
  513.5 1.1 broadcast_multiply_fusion
  514.6 0.8 copy.28
  515.4 0.8 copy.29
  516.2 0.0 copy-done.6
  516.3 0.6 broadcast_multiply_fusion.2
  (8 shorter events, 0.1 us)
Async XLA Ops:
  7.2 0.9 copy-start
  14.6 13.5 %copy-start.7 = (s32[1,64,64]{2,1,0:T(8,128)S(1)}, s32[1,64,64]{2,1,0:T(8,128)}, u32[]{:S(2)}) copy-start(s32[1,64,64]{2,1,0:T(8,128)} %param.8) | copy-start | bytes 49156
  14.6 13.8 %copy-start.8 = (bf16[256,64]{0,1:T(8,128)(2,1)S(1)}, bf16[256,64]{0,1:T(8,128)(2,1)}, u32[]{:S(2)}) copy-start(bf16[256,64]{0,1:T(8,128)(2,1)} %param.11) | copy-start | bytes 98308
  14.6 14.0 %copy-start.4 = (bf16[1,256,256]{2,1,0:T(8,128)(2,1)S(1)}, bf16[1,256,256]{2,1,0:T(8,128)(2,1)}, u32[]{:S(2)}) copy-start(bf16[1,256,256]{2,1,0:T(8,128)(2,1)} %param.13) | copy-start | bytes 393220
  14.6 14.0 %copy-start.5 = (bf16[256,256]{1,0:T(8,128)(2,1)S(1)}, bf16[256,256]{1,0:T(8,128)(2,1)}, u32[]{:S(2)}) copy-start(bf16[256,256]{1,0:T(8,128)(2,1)} %param.12) | copy-start | bytes 393220
  14.6 195.9 %all-to-all-start = ((bf16[64,1,16,32,128]{4,3,2,1,0:T(8,128)(2,1)}), bf16[64,1,16,32,128]{4,3,2,1,0:T(8,128)(2,1)}, u32[]{:S(2)}, u32[]{:S(2)}) async-start(bf16[64,1,16,32,128]{4,3,2,1,0:T(8,128)(2,1)} %stack.3), calls=%async_computation | async-start | bytes 16777216 | tf_op jit(solution)/shard_map/all_to_all | solution.py:48
  214.6 5.3 %copy-start.1 = (bf16[1,64,256,128]{3,2,1,0:T(8,128)(2,1)S(1)}, bf16[1,64,256,128]{3,2,1,0:T(8,128)(2,1)}, u32[]{:S(2)}) copy-start(bf16[1,64,256,128]{3,2,1,0:T(8,128)(2,1)} %param.9) | copy-start | bytes 12582916
  224.5 11.3 %copy-start.2 = (f32[64,32,256]{2,1,0:T(8,128)S(1)}, f32[64,32,256]{2,1,0:T(8,128)}, u32[]{:S(2)}) copy-start(f32[64,32,256]{2,1,0:T(8,128)} %get-tuple-element.27) | copy-start | bytes 6291460
  224.5 38.2 %all-to-all-start.1 = ((bf16[64,2,32,128]{3,2,1,0:T(8,128)(2,1)}), bf16[64,2,32,128]{3,2,1,0:T(8,128)(2,1)S(1)}, u32[]{:S(2)}, u32[]{:S(2)}) async-start(bf16[64,2,32,128]{3,2,1,0:T(8,128)(2,1)} %bitcast.27), calls=%async_computation.1 | async-start | bytes 2097152 | tf_op jit(solution)/shard_map/all_to_all | solution.py:90
  234.7 278.8 %all-reduce.3.cloned.1.call-start = ((), (), s32[]{:S(2)}) async-start(), calls=%async_computation.2 | async-start | bytes 1179648 | tf_op jit(solution)/shard_map/psum | solution.py:113
  263.1 2.2 copy-start.9
  263.2 2.4 copy-start.3
  513.5 2.8 copy-start.6
Sparse Core Ops, SparseCore 0:
  265.4 247.9 all-reduce.2
